TPU v7x, 256 devices: a whole 4x4x8 slice. The times are simulated.
256 devices in a mesh: tile: 16 (over z, core), lev: 4 (over x), tag: 4 (over y).
Axes of the slice: x: 4, y: 4, z: 8, core: 2. Of those that a mesh axis runs over, the one named last changes fastest.
Arguments:
- parent_field: float32 [8, 32, 256, 1024], P('tag', 'lev', 'tile'), may hold values from -6 to 6
- nest_field: float32 [8, 32, 256, 1024], P('tag', 'lev', 'tile'), may hold values from -6 to 6
- parent_mixing: float32 [32, 256, 1024], P('lev', 'tile'), may hold values from 0.05 to 5
- parent_eastward: float32 [256, 1024], P('tile'), may hold values from 0.02 to 0.12
- parent_northward: float32 [256, 1024], P('tile'), may hold values from 0.02 to 0.12
- nest_eastward: float32 [256, 1024], P('tile'), may hold values from 0.02 to 0.12
- nest_northward: float32 [256, 1024], P('tile'), may hold values from 0.02 to 0.12
- strip_tile: int32 [16, 256], replicated, may hold values from 0 to 15, as said below
- strip_block: int32 [16, 256], replicated, may hold values from 0 to 127
- strip_target: int32 [16, 256], replicated, may hold values from 0 to 127
- strip_count: int32 [16], replicated, may hold values from 1 to 256, as said below
Outputs:
- parent_adjoint: float32 [8, 32, 256, 1024], P('tag', 'lev', 'tile')
- nest_adjoint: float32 [8, 32, 256, 1024], P('tag', 'lev', 'tile')
- bulk_adjoint: float32 [32, 256, 1024], P('lev', 'tile', 'tag')
Inputs may be any that keep to these rules, and one draw needn't show every extreme that they name: `strip_tile`: among the first strip_count[j] entries of row j, every parent tile appears at most 16 times; in the row whose count is 256 every parent tile appears exactly 16 times. `strip_count`: exactly one nest tile lists 256 strips; every other lists at most 128.
All inputs are finite; a program needn't handle non-finite values.
Results may differ from a plain program's by a relative error of at most 0.0003.
Values sent between devices are 32-bit elements; how exact they have to be, the bound alone decides.
A program may use at most 64 MiB of HBM per device.

v0:
```python
import jax
import jax.numpy as jnp
from jax import lax
from jax.sharding import PartitionSpec as P

CAP = 16
NSUB = 3
HIGHEST = lax.Precision.HIGHEST


def extended(cells, sides, width):
    for axis, dim in sides:
        count = lax.axis_size(axis)
        ends = count - 1
        head = lax.slice_in_dim(cells, 0, width, axis=dim)
        tail = lax.slice_in_dim(cells, cells.shape[dim] - width, cells.shape[dim], axis=dim)
        cells = jnp.concatenate(
            [
                lax.ppermute(tail, axis, [(i, (i + 1) % count) for i in range(ends)]),
                cells,
                lax.ppermute(head, axis, [((i + 1) % count, i) for i in range(ends)]),
            ],
            axis=dim,
        )
    return cells


def tridiagonal(source, mixing):
    level_count = mixing.shape[0]
    mixing_up = jnp.concatenate([mixing[1:], jnp.zeros_like(mixing[:1])], axis=0)
    diagonal = 1.0 + mixing + mixing_up
    ratio_now = jnp.zeros_like(mixing[0])
    carry_now = jnp.zeros_like(source[:, 0])
    ratios = []
    carries = []
    for lev_index in range(level_count):
        pivot_now = diagonal[lev_index] + mixing[lev_index] * ratio_now
        ratio_now = -mixing_up[lev_index] / pivot_now
        carry_now = (source[:, lev_index] + mixing[lev_index] * carry_now) / pivot_now
        ratios.append(ratio_now)
        carries.append(carry_now)
    value_now = carries[level_count - 1]
    results = [value_now]
    for lev_index in range(level_count - 2, -1, -1):
        value_now = carries[lev_index] - ratios[lev_index] * value_now
        results.append(value_now)
    return jnp.stack(results[::-1], axis=1)


def relax(padded, eastward):
    center = padded[:-1, 1:-1]
    row_above = padded[:-1, :-2]
    row_below = padded[:-1, 2:]
    north_here = padded[-1, 1:-1]
    north_above = padded[-1, :-2]
    zero_column = jnp.zeros_like(center[:, :, :1])
    east_cell = jnp.concatenate([center[:, :, 1:], zero_column], axis=2)
    west_cell = jnp.concatenate([zero_column, center[:, :, :-1]], axis=2)
    west_rate = jnp.concatenate([jnp.zeros_like(eastward[:, :1]), eastward[:, :-1]], axis=1)
    return (
        center
        + north_here * (row_below - center)
        + north_above * (row_above - center)
        + eastward * (east_cell - center)
        + west_rate * (west_cell - center)
    )


def rims(stacked):
    return extended(stacked, (("tile", 1),), 1)


def advance(start, solved, parent_eastward, parent_northward, nest_eastward, nest_northward):
    tag_count, level_count, row_count, col_count = start.shape
    line_count = tag_count * level_count
    nest_now = start.reshape(line_count, row_count, col_count)
    parent_now = solved.reshape(line_count, row_count, col_count)
    for sub_step in range(NSUB):
        nest_stack = jnp.concatenate([nest_now, nest_northward[None]], axis=0)
        if sub_step == 0:
            parent_stack = jnp.concatenate([parent_now, parent_northward[None]], axis=0)
            padded = rims(jnp.concatenate([parent_stack, nest_stack], axis=0))
            parent_now = relax(padded[: line_count + 1], parent_eastward)
            nest_now = relax(padded[line_count + 1 :], nest_eastward)
        else:
            nest_now = relax(rims(nest_stack), nest_eastward)
    full_shape = (tag_count, level_count, row_count, col_count)
    return (parent_now.reshape(full_shape), nest_now.reshape(full_shape))


def deliver(parent_field, strip_tile, strip_block, strip_target, strip_count):
    tag_count, level_count, row_count, col_count = parent_field.shape
    line_count = tag_count * level_count
    block_count = row_count * col_count // 128
    tile_count, slot_total = strip_tile.shape
    own_index = lax.axis_index("tile")
    positions = jnp.arange(slot_total, dtype=jnp.int32)
    is_live = positions[None, :] < strip_count[:, None]
    from_here = jnp.logical_and(is_live, strip_tile == own_index).astype(jnp.int32)
    slot_rank = jnp.cumsum(from_here, axis=1) - 1
    slot_index = jnp.arange(CAP, dtype=jnp.int32)
    select = from_here[:, None, :] * (slot_rank[:, None, :] == slot_index[None, :, None]).astype(
        jnp.int32
    )
    source_block = jnp.sum(select * strip_block[:, None, :], axis=2).reshape(-1)
    filled = jnp.sum(select, axis=2).reshape(-1).astype(jnp.float32)
    blocks = parent_field.reshape(line_count, block_count, 128)
    packed = jnp.take(blocks, source_block, axis=1) * filled[None, :, None]
    received = lax.all_to_all(packed, "tile", split_axis=1, concat_axis=1, tiled=True)
    own_tile = lax.dynamic_index_in_dim(strip_tile, own_index, 0, keepdims=False)
    own_target = lax.dynamic_index_in_dim(strip_target, own_index, 0, keepdims=False)
    own_count = lax.dynamic_index_in_dim(strip_count, own_index, 0, keepdims=False)
    own_live = (positions < own_count).astype(jnp.int32)
    from_source = (own_tile[:, None] == jnp.arange(tile_count, dtype=jnp.int32)[None, :]).astype(
        jnp.int32
    ) * own_live[:, None]
    own_rank = jnp.sum((jnp.cumsum(from_source, axis=0) - 1) * from_source, axis=1)
    arrival = own_tile * CAP + own_rank
    pick_slot = (arrival[:, None] == jnp.arange(tile_count * CAP, dtype=jnp.int32)[None, :]).astype(
        jnp.float32
    )
    pick_slot = pick_slot * own_live[:, None].astype(jnp.float32)
    place_block = (own_target[:, None] == jnp.arange(block_count, dtype=jnp.int32)[None, :]).astype(
        jnp.float32
    )
    routing = jnp.dot(pick_slot.T, place_block, precision=HIGHEST)
    forcing = jnp.einsum("lic,ib->lbc", received, routing, precision=HIGHEST)
    return forcing.reshape(tag_count, level_count, row_count, col_count)


def shards(
    parent_field,
    nest_field,
    parent_mixing,
    parent_eastward,
    parent_northward,
    nest_eastward,
    nest_northward,
    strip_tile,
    strip_block,
    strip_target,
    strip_count,
):
    tag_count = parent_field.shape[0]
    forcing = deliver(parent_field, strip_tile, strip_block, strip_target, strip_count)
    stacked = jnp.concatenate([parent_field, parent_mixing[None]], axis=0)
    columns = lax.all_to_all(stacked, "lev", split_axis=3, concat_axis=1, tiled=True)
    column_result = tridiagonal(columns[:tag_count], columns[tag_count])
    solved = lax.all_to_all(column_result, "lev", split_axis=1, concat_axis=3, tiled=True)
    parent_adjoint, nest_adjoint = advance(
        nest_field + forcing,
        solved,
        parent_eastward,
        parent_northward,
        nest_eastward,
        nest_northward,
    )
    bulk_adjoint = lax.psum_scatter(
        jnp.sum(parent_adjoint, axis=0), "tag", scatter_dimension=2, tiled=True
    )
    return (parent_adjoint, nest_adjoint, bulk_adjoint)


def solution(mesh):
    in_specs = (
        P("tag", "lev", "tile", None),
        P("tag", "lev", "tile", None),
        P("lev", "tile", None),
        P("tile", None),
        P("tile", None),
        P("tile", None),
        P("tile", None),
        P(),
        P(),
        P(),
        P(),
    )
    out_specs = (
        P("tag", "lev", "tile", None),
        P("tag", "lev", "tile", None),
        P("lev", "tile", "tag"),
    )
    return jax.shard_map(shards, mesh=mesh, in_specs=in_specs, out_specs=out_specs, check_vma=False)
```

profile of v0, /device:TPU:2, one launch (start us, length us, event | category | flops | bytes accessed | tf_op | source)
XLA Modules:
  0.0 209.8 jit_solution(3081090923372214536)
XLA Ops:
  7.2 1.5 pad_maximum_fusion.5
  8.7 6.9 %copy.55 = f32[3,8,16,1024]{2,1,0,3:T(8,128)} copy(f32[3,8,16,1024]{3,2,1,0:T(8,128)S(1)} %pad_maximum_fusion.5) | data formatting | bytes 3145728 | tf_op jit(solution)/shard_map/concatenate | solution.py:146
  15.6 8.3 %reshape.176 = f32[4,1,98304]{2,1,0:T(1,128)} reshape(f32[1024,3,8,16]{3,2,1,0:T(8,128)} %bitcast.230) | data formatting | bytes 3145728
  23.9 5.9 %all-to-all-start = ((f32[4,1,98304]{2,1,0:T(1,128)}), f32[4,1,98304]{2,1,0:T(1,128)S(1)}, u32[]{:S(2)}, u32[]{:S(2)}) async-start(f32[4,1,98304]{2,1,0:T(1,128)} %reshape.176), calls=%async_computation | async-start | bytes 3145728 | tf_op jit(solution)/shard_map/all_to_all | solution.py:147
  32.7 1.8 copy.65
  34.7 13.4 %all-to-all-done = f32[4,1,98304]{2,1,0:T(1,128)S(1)} async-done(((f32[4,1,98304]{2,1,0:T(1,128)}), f32[4,1,98304]{2,1,0:T(1,128)S(1)}, u32[]{:S(2)}, u32[]{:S(2)}) %all-to-all-start) | async-done | bytes 1572896 | tf_op jit(solution)/shard_map/all_to_all | solution.py:147
  48.1 1.2 copy-done.1
  49.8 6.2 %reduce.4 = f32[4,98304]{1,0:T(4,128)S(1)} reduce(f32[4,1,98304]{2,1,0:T(1,128)} %copy-done.1, f32[]{:T(128)} %broadcast.2764), dimensions={1}, to_apply=%all_to_all.25.reduce_sub_computation | reduce | bytes 3145732 | tf_op jit(solution)/shard_map/all_to_all | solution.py:147
  55.9 8.9 %reshape.177 = f32[1024,3,8,16]{3,2,1,0:T(8,128)} reshape(f32[4,98304]{1,0:T(4,128)S(1)} %reduce.4) | data formatting | bytes 3145728
  64.8 7.8 %copy.69 = f32[3,8,16,4,256]{4,3,2,1,0:T(4,128)S(1)} copy(f32[3,8,16,4,256]{2,1,0,4,3:T(8,128)} %bitcast.231) | data formatting | bytes 3145728 | tf_op jit(solution)/shard_map/all_to_all | solution.py:147
  75.9 5.7 %all-to-all-start.1 = ((f32[2,32,16,256]{3,2,0,1:T(8,128)}), f32[2,32,16,256]{3,2,0,1:T(8,128)}, u32[]{:S(2)}, u32[]{:S(2)}) async-start(f32[2,32,16,256]{3,2,0,1:T(8,128)} %copy.59), calls=%async_computation.1 | async-start | bytes 2097152 | tf_op jit(solution)/shard_map/all_to_all | solution.py:149
  82.6 2.5 %multiply_bitcast_fusion = f32[16,256,128]{2,0,1:T(8,128)} fusion(f32[256,16,128]{2,1,0:T(8,128)S(1)} %gather_fusion, f32[256]{0:T(256)S(1)} %convert_element_type.43, pred[256]{0:T(512)(128)(4,1)S(1)} %compare_and_fusion), kind=kLoop, calls=%fused_computation.5 | loop fusion | flops 1048576 | bytes 4195584 | tf_op jit(solution)/shard_map/mul | solution.py:108
  85.2 8.3 %all-to-all-done.1 = f32[2,32,16,256]{3,2,0,1:T(8,128)} async-done(((f32[2,32,16,256]{3,2,0,1:T(8,128)}), f32[2,32,16,256]{3,2,0,1:T(8,128)}, u32[]{:S(2)}, u32[]{:S(2)}) %all-to-all-start.1) | async-done | bytes 1048608 | tf_op jit(solution)/shard_map/all_to_all | solution.py:149
  93.4 9.6 %all-to-all-start.2 = ((f32[16,256,128]{2,0,1:T(8,128)}), f32[16,256,128]{2,0,1:T(8,128)}, u32[]{:S(2)}, u32[]{:S(2)}) async-start(f32[16,256,128]{2,0,1:T(8,128)} %multiply_bitcast_fusion), calls=%async_computation.2 | async-start | bytes 4194304 | tf_op jit(solution)/shard_map/all_to_all | solution.py:109
  107.9 1.9 copy.61
  110.4 1.7 fusion.137
  112.1 40.2 %all-to-all-done.2 = f32[16,256,128]{2,0,1:T(8,128)} async-done(((f32[16,256,128]{2,0,1:T(8,128)}), f32[16,256,128]{2,0,1:T(8,128)}, u32[]{:S(2)}, u32[]{:S(2)}) %all-to-all-start.2) | async-done | bytes 2097184 | tf_op jit(solution)/shard_map/all_to_all | solution.py:109
  152.3 3.4 %fusion.4 = f32[16,128,128]{2,1,0:T(8,128)S(1)} fusion(f32[256,128,1]{0,1,2:T(8,128)S(1)} %convolution_bitcast_fusion, f32[16,256,128]{2,0,1:T(8,128)} %all-to-all-done.2), kind=kOutput, calls=%fused_computation.12 | convolution fusion | flops 805306368 | bytes 3276800 | tf_op jit(solution)/shard_map/lic,ib->lbc/dot_general | solution.py:127
  155.9 1.4 add.2442
  157.5 2.1 collective-permute-start.1
  159.6 1.3 collective-permute-start
  161.3 1.5 collective-permute-done
  163.6 1.7 fusion.135
  165.4 5.2 %collective-permute-start.3 = (f32[17,1,1024]{2,1,0:T(1,128)S(1)}, f32[17,1,1024]{2,1,0:T(1,128)S(1)}, u32[]{:S(2)}, u32[]{:S(2)}) collective-permute-start(f32[17,1,1024]{2,1,0:T(1,128)S(1)} %get-tuple-element.88), channel_id=1, source_target_pairs={{0,16},{16,32},{32,48},{48,64},{64,80},{80,96},{96,112},{112,128},... | collective-permute-start | bytes 208904 | tf_op jit(solution)/shard_map/ppermute | solution.py:19
  170.7 1.5 collective-permute-start.2
  172.2 1.7 fusion.35
  173.9 2.1 %reduce_sum.39 = f32[8,16,1024]{2,1,0:T(8,128)} reduce(f32[2,8,16,1024]{3,2,1,0:T(8,128)} %bitcast.265, f32[]{:T(128)} %constant.48.clone.1), dimensions={0}, to_apply=%region_7.8 | reduce | flops 131072 | bytes 1572868 | tf_op jit(solution)/shard_map/reduce_sum | solution.py:159
  178.4 3.0 %collective-permute-start.5 = (f32[17,1,1024]{2,1,0:T(1,128)S(1)}, f32[17,1,1024]{2,1,0:T(1,128)S(1)}, u32[]{:S(2)}, u32[]{:S(2)}) collective-permute-start(f32[17,1,1024]{2,1,0:T(1,128)S(1)} %get-tuple-element.86), channel_id=1, source_target_pairs={{0,16},{16,32},{32,48},{48,64},{64,80},{80,96},{96,112},{112,128},... | collective-permute-start | bytes 208904 | tf_op jit(solution)/shard_map/ppermute | solution.py:19
  181.8 1.3 collective-permute-start.4
  183.4 2.3 %collective-permute-done.4 = f32[17,1,1024]{2,1,0:T(1,128)S(1)} collective-permute-done((f32[17,1,1024]{2,1,0:T(1,128)S(1)}, f32[17,1,1024]{2,1,0:T(1,128)S(1)}, u32[]{:S(2)}, u32[]{:S(2)}) %collective-permute-start.4) | collective-permute-done | bytes 69664 | tf_op jit(solution)/shard_map/ppermute | solution.py:21
  185.7 1.6 fusion.27
  187.3 15.6 %reduce-scatter.2.cloned.1.call-done = f32[8,16,256]{2,1,0:T(8,128)} async-done(((f32[8,16,1024]{2,1,0:T(8,128)}), f32[8,16,256]{2,1,0:T(8,128)}) %reduce-scatter.2.cloned.1.call-update) | async-done | bytes 131088 | tf_op jit(solution)/shard_map/reduce_scatter | solution.py:158
  (134 shorter events, 17.3 us)
Async XLA Ops:
  23.9 5.9 %copy-start.2 = (f32[2,8,16,1024]{3,2,1,0:T(8,128)S(1)}, f32[2,8,16,1024]{3,2,1,0:T(8,128)}, u32[]{:S(2)}) copy-start(f32[2,8,16,1024]{3,2,1,0:T(8,128)} %param.11) | copy-start | bytes 3145732
  23.9 24.2 %all-to-all-start = ((f32[4,1,98304]{2,1,0:T(1,128)}), f32[4,1,98304]{2,1,0:T(1,128)S(1)}, u32[]{:S(2)}, u32[]{:S(2)}) async-start(f32[4,1,98304]{2,1,0:T(1,128)} %reshape.176), calls=%async_computation | async-start | bytes 3145728 | tf_op jit(solution)/shard_map/all_to_all | solution.py:147
  29.8 1.1 copy-start.10
  29.8 1.1 copy-start.12
  29.8 2.2 %copy-start.11 = (s32[16,256]{1,0:T(8,128)S(1)}, s32[16,256]{1,0:T(8,128)}, u32[]{:S(2)}) copy-start(s32[16,256]{1,0:T(8,128)} %param.19) | copy-start | bytes 49156
  48.1 1.2 copy-start.1
  75.9 17.5 %all-to-all-start.1 = ((f32[2,32,16,256]{3,2,0,1:T(8,128)}), f32[2,32,16,256]{3,2,0,1:T(8,128)}, u32[]{:S(2)}, u32[]{:S(2)}) async-start(f32[2,32,16,256]{3,2,0,1:T(8,128)} %copy.59), calls=%async_computation.1 | async-start | bytes 2097152 | tf_op jit(solution)/shard_map/all_to_all | solution.py:149
  85.2 20.7 %copy-start.8 = (f32[16,1024]{1,0:T(8,128)S(1)}, f32[16,1024]{1,0:T(8,128)}, u32[]{:S(2)}) copy-start(f32[16,1024]{1,0:T(8,128)} %param.16) | copy-start | bytes 196612
  85.2 20.8 %copy-start.9 = (f32[16,1024]{1,0:T(8,128)S(1)}, f32[16,1024]{1,0:T(8,128)}, u32[]{:S(2)}) copy-start(f32[16,1024]{1,0:T(8,128)} %param.14) | copy-start | bytes 196612
  93.4 58.9 %all-to-all-start.2 = ((f32[16,256,128]{2,0,1:T(8,128)}), f32[16,256,128]{2,0,1:T(8,128)}, u32[]{:S(2)}, u32[]{:S(2)}) async-start(f32[16,256,128]{2,0,1:T(8,128)} %multiply_bitcast_fusion), calls=%async_computation.2 | async-start | bytes 4194304 | tf_op jit(solution)/shard_map/all_to_all | solution.py:109
  103.0 99.9 %reduce-scatter.2.cloned.1.call-start = ((), (), s32[]{:S(2)}) async-start(), calls=%async_computation.4 | async-start | bytes 655360 | tf_op jit(solution)/shard_map/reduce_scatter | solution.py:158
  155.8 1.4 copy-start
  155.8 1.4 copy-start.7
  157.5 3.8 %collective-permute-start.1 = (f32[34,1,1024]{2,1,0:T(1,128)S(1)}, f32[34,1,1024]{2,1,0:T(1,128)S(1)}, u32[]{:S(2)}, u32[]{:S(2)}) collective-permute-start(f32[34,1,1024]{2,1,0:T(1,128)S(1)} %get-tuple-element.84), channel_id=1, source_target_pairs={{0,16},{16,32},{32,48},{48,64},{64,80},{80,96},{96,112},{112,128},... | collective-permute-start | bytes 417800 | tf_op jit(solution)/shard_map/ppermute | solution.py:19
  159.6 3.3 %collective-permute-start = (f32[34,1,1024]{2,1,0:T(1,128)S(1)}, f32[34,1,1024]{2,1,0:T(1,128)S(1)}, u32[]{:S(2)}, u32[]{:S(2)}) collective-permute-start(f32[34,1,1024]{2,1,0:T(1,128)S(1)} %get-tuple-element.83), channel_id=1, source_target_pairs={{16,0},{32,16},{48,32},{64,48},{80,64},{96,80},{112,96},{128,112},... | collective-permute-start | bytes 417800 | tf_op jit(solution)/shard_map/ppermute | solution.py:21
  163.6 8.6 %copy-start.6 = (f32[16,16,1023]{2,1,0:T(8,128)S(1)}, f32[16,16,1023]{2,1,0:T(8,128)}, u32[]{:S(2)}) copy-start(f32[16,16,1023]{2,1,0:T(8,128)} %get-tuple-element.96) | copy-start | bytes 3142660
  165.3 6.9 %copy-start.5 = (f32[16,16,1023]{2,1,0:T(8,128)S(1)}, f32[16,16,1023]{2,1,0:T(8,128)}, u32[]{:S(2)}) copy-start(f32[16,16,1023]{2,1,0:T(8,128)} %get-tuple-element.95) | copy-start | bytes 3142660
  165.4 10.7 %collective-permute-start.3 = (f32[17,1,1024]{2,1,0:T(1,128)S(1)}, f32[17,1,1024]{2,1,0:T(1,128)S(1)}, u32[]{:S(2)}, u32[]{:S(2)}) collective-permute-start(f32[17,1,1024]{2,1,0:T(1,128)S(1)} %get-tuple-element.88), channel_id=1, source_target_pairs={{0,16},{16,32},{32,48},{48,64},{64,80},{80,96},{96,112},{112,128},... | collective-permute-start | bytes 208904 | tf_op jit(solution)/shard_map/ppermute | solution.py:19
  170.7 5.7 %collective-permute-start.2 = (f32[17,1,1024]{2,1,0:T(1,128)S(1)}, f32[17,1,1024]{2,1,0:T(1,128)S(1)}, u32[]{:S(2)}, u32[]{:S(2)}) collective-permute-start(f32[17,1,1024]{2,1,0:T(1,128)S(1)} %get-tuple-element.87), channel_id=1, source_target_pairs={{16,0},{32,16},{48,32},{64,48},{80,64},{96,80},{112,96},{128,112},... | collective-permute-start | bytes 208904 | tf_op jit(solution)/shard_map/ppermute | solution.py:21
  176.1 1.2 copy-start.3
  176.1 1.5 copy-start.4
  178.4 4.7 %collective-permute-start.5 = (f32[17,1,1024]{2,1,0:T(1,128)S(1)}, f32[17,1,1024]{2,1,0:T(1,128)S(1)}, u32[]{:S(2)}, u32[]{:S(2)}) collective-permute-start(f32[17,1,1024]{2,1,0:T(1,128)S(1)} %get-tuple-element.86), channel_id=1, source_target_pairs={{0,16},{16,32},{32,48},{48,64},{64,80},{80,96},{96,112},{112,128},... | collective-permute-start | bytes 208904 | tf_op jit(solution)/shard_map/ppermute | solution.py:19
  181.8 3.9 %collective-permute-start.4 = (f32[17,1,1024]{2,1,0:T(1,128)S(1)}, f32[17,1,1024]{2,1,0:T(1,128)S(1)}, u32[]{:S(2)}, u32[]{:S(2)}) collective-permute-start(f32[17,1,1024]{2,1,0:T(1,128)S(1)} %get-tuple-element.85), channel_id=1, source_target_pairs={{16,0},{32,16},{48,32},{64,48},{80,64},{96,80},{112,96},{128,112},... | collective-permute-start | bytes 208904 | tf_op jit(solution)/shard_map/ppermute | solution.py:21
Sparse Core Ops, SparseCore 0:
  176.2 26.7 reduce-scatter.1
where the time goes:
time: 211 us; the launch traced here: 210 us
  waiting for transfers between devices  81.3 us (39%)
  local copies, waits for them, and re-layouts  49.5 us (23%)
  starting transfers between devices  35.7 us (17%)
  other arithmetic  24.7 us (12%)
  between operations  14.8 us (7%)
  matrix products  3.79 us (2%)
    all_to_all x1, waiting for transfers between devices, deliver(): lax.all_to_all(packed, 'tile', split_axis=1, concat_axis=1, tiled=True)  40.2 us
    unnamed x43, local copies, waits for them, and re-layouts  19.7 us
    reduce_scatter x1, waiting for transfers between devices, shards(): lax.psum_scatter(jnp.sum(parent_adjoint, axis=0), 'tag', scatter_dimensio...  15.6 us
    all_to_all x1, waiting for transfers between devices, shards(): lax.all_to_all(stacked, 'lev', split_axis=3, concat_axis=1, tiled=True)  13.4 us
    ppermute x3, starting transfers between devices, extended(): lax.ppermute(tail, axis, [(i, (i + 1) % count) for i in range(ends)])  10.3 us
    all_to_all x1, starting transfers between devices, deliver(): lax.all_to_all(packed, 'tile', split_axis=1, concat_axis=1, tiled=True)  9.61 us
    all_to_all x2, local copies, waits for them, and re-layouts, shards(): lax.all_to_all(stacked, 'lev', split_axis=3, concat_axis=1, tiled=True)  8.35 us
    all_to_all x1, waiting for transfers between devices, shards(): lax.all_to_all(column_result, 'lev', split_axis=1, concat_axis=3, tiled=T...  8.27 us
  transfers between devices with their start and end apart: 10, of which 6 were waited for; matrix products, arithmetic and copies ran while one was open for 12% of the time, Pallas kernels for 0%

commit v1 on v0

--- a/solution.py
+++ b/solution.py
@@ -6,6 +6,30 @@
 CAP = 16
 NSUB = 3
 HIGHEST = lax.Precision.HIGHEST
+
+
+def split_up(shard, dim, devices):
+    dims = shard.shape
+    blocks = shard.reshape(*dims[:dim], devices, dims[dim] // devices, *dims[dim + 1 :])
+    return jnp.moveaxis(blocks, dim, 0)
+
+
+def laid_out(blocks, dim):
+    dims = list(blocks.shape[1:])
+    dims[dim] *= blocks.shape[0]
+    return jnp.moveaxis(blocks, 0, dim).reshape(dims)
+
+
+def exchange_directly(shard, axis, split_dim, concat_dim):
+    size, mine = (lax.axis_size(axis), lax.axis_index(axis))
+    blocks = split_up(shard, split_dim, size)
+    filled = blocks
+    for lap in range(1, size):
+        target, source = ((mine + lap) % size, (mine - lap) % size)
+        sent = lax.dynamic_index_in_dim(blocks, target, 0)
+        theirs = lax.ppermute(sent, axis, [(i, (i + lap) % size) for i in range(size)])
+        filled = lax.dynamic_update_slice_in_dim(filled, theirs, source, axis=0)
+    return laid_out(filled, concat_dim)
 
 
 def extended(cells, sides, width):
@@ -146,7 +170,7 @@
     stacked = jnp.concatenate([parent_field, parent_mixing[None]], axis=0)
     columns = lax.all_to_all(stacked, "lev", split_axis=3, concat_axis=1, tiled=True)
     column_result = tridiagonal(columns[:tag_count], columns[tag_count])
-    solved = lax.all_to_all(column_result, "lev", split_axis=1, concat_axis=3, tiled=True)
+    solved = exchange_directly(column_result, "lev", 1, 3)
     parent_adjoint, nest_adjoint = advance(
         nest_field + forcing,
         solved,

time: 211 us -> 174 us (0.82)
  waiting for transfers between devices: 81.3 us -> 38.9 us
  local copies, waits for them, and re-layouts: 49.5 us -> 54.1 us
    all_to_all x1, waiting for transfers between devices: 40.2 us -> 0.01 us  [deliver(): lax.all_to_all(packed, 'tile', split_axis=1, concat_axis=1, tiled=True)]
    ppermute x0 -> x3, waiting for transfers between devices: none -> 8.38 us  [exchange_directly(): lax.ppermute(sent, axis, [(i, (i + lap) % size) for i in range(size)])]
    all_to_all x1 -> x0, waiting for transfers between devices: 8.27 us -> none  [shards(): lax.all_to_all(column_result, 'lev', split_axis=1, concat_axis=3, tiled=T...]
    all_to_all x1 -> x0, starting transfers between devices: 5.69 us -> none  [shards(): lax.all_to_all(column_result, 'lev', split_axis=1, concat_axis=3, tiled=T...]
    all_to_all x1, waiting for transfers between devices: 13.4 us -> 7.95 us  [shards(): lax.all_to_all(stacked, 'lev', split_axis=3, concat_axis=1, tiled=True)]
    ppermute x0 -> x3, starting transfers between devices: none -> 4.17 us  [exchange_directly(): lax.ppermute(sent, axis, [(i, (i + lap) % size) for i in range(size)])]
    dynamic_update_slice x0 -> x3, local copies, waits for them, and re-layouts: none -> 2.9 us  [exchange_directly(): filled = lax.dynamic_update_slice_in_dim(filled, theirs, source, axis=0)]
    reduce_scatter x1, waiting for transfers between devices: 15.6 us -> 18.1 us  [shards(): lax.psum_scatter(jnp.sum(parent_adjoint, axis=0), 'tag', scatter_dimensio...]
  transfers between devices with their start and end apart: 10 -> 12, of which waited for: 6 -> 7; matrix products, arithmetic and copies ran while one was open for 12% -> 34% of each run, Pallas kernels for 0% -> 0%
where the time goes in v1:
time: 174 us; the launch traced here: 173 us
  local copies, waits for them, and re-layouts  54.1 us (31%)
  waiting for transfers between devices  38.9 us (22%)
  starting transfers between devices  34.8 us (20%)
  other arithmetic  26 us (15%)
  between operations  14.7 us (8%)
  matrix products  4.75 us (3%)
    unnamed x43, local copies, waits for them, and re-layouts  19.8 us
    reduce_scatter x1, waiting for transfers between devices, shards(): lax.psum_scatter(jnp.sum(parent_adjoint, axis=0), 'tag', scatter_dimensio...  18.1 us
    ppermute x3, starting transfers between devices, extended(): lax.ppermute(tail, axis, [(i, (i + 1) % count) for i in range(ends)])  11.1 us
    all_to_all x2, local copies, waits for them, and re-layouts, shards(): lax.all_to_all(stacked, 'lev', split_axis=3, concat_axis=1, tiled=True)  9.06 us
    all_to_all x1, starting transfers between devices, deliver(): lax.all_to_all(packed, 'tile', split_axis=1, concat_axis=1, tiled=True)  8.76 us
    ppermute x3, waiting for transfers between devices, exchange_directly(): lax.ppermute(sent, axis, [(i, (i + lap) % size) for i in range(size)])  8.38 us
    all_to_all x1, waiting for transfers between devices, shards(): lax.all_to_all(stacked, 'lev', split_axis=3, concat_axis=1, tiled=True)  7.95 us
    all_to_all x1, other arithmetic, shards(): lax.all_to_all(stacked, 'lev', split_axis=3, concat_axis=1, tiled=True)  7.31 us
  transfers between devices with their start and end apart: 12, of which 7 were waited for; matrix products, arithmetic and copies ran while one was open for 34% of the time, Pallas kernels for 0%

profile of v1, /device:TPU:2, one launch (start us, length us, event | category | flops | bytes accessed | tf_op | source)
XLA Modules:
  0.0 173.4 jit_solution(16299069669201103449)
XLA Ops:
  7.2 1.5 pad_maximum_fusion.5
  8.7 7.0 %copy.51 = f32[3,8,16,1024]{2,1,0,3:T(8,128)} copy(f32[3,8,16,1024]{3,2,1,0:T(8,128)S(1)} %pad_maximum_fusion.5) | data formatting | bytes 3145728 | tf_op jit(solution)/shard_map/concatenate | solution.py:170
  15.6 8.3 %reshape.178 = f32[4,1,98304]{2,1,0:T(1,128)} reshape(f32[1024,3,8,16]{3,2,1,0:T(8,128)} %bitcast.237) | data formatting | bytes 3145728
  23.9 6.7 %all-to-all-start = ((f32[4,1,98304]{2,1,0:T(1,128)}), f32[4,1,98304]{2,1,0:T(1,128)}, u32[]{:S(2)}, u32[]{:S(2)}) async-start(f32[4,1,98304]{2,1,0:T(1,128)} %reshape.178), calls=%async_computation | async-start | bytes 3145728 | tf_op jit(solution)/shard_map/all_to_all | solution.py:171
  37.9 2.5 %multiply_bitcast_fusion = f32[16,256,128]{2,0,1:T(8,128)} fusion(f32[256,16,128]{2,1,0:T(8,128)S(1)} %gather_fusion, f32[256]{0:T(256)S(1)} %convert_element_type.43, pred[256]{0:T(512)(128)(4,1)S(1)} %compare_and_fusion), kind=kLoop, calls=%fused_computation.5 | loop fusion | flops 1048576 | bytes 4195584 | tf_op jit(solution)/shard_map/mul | solution.py:132
  40.4 7.9 %all-to-all-done = f32[4,1,98304]{2,1,0:T(1,128)} async-done(((f32[4,1,98304]{2,1,0:T(1,128)}), f32[4,1,98304]{2,1,0:T(1,128)}, u32[]{:S(2)}, u32[]{:S(2)}) %all-to-all-start) | async-done | bytes 1572896 | tf_op jit(solution)/shard_map/all_to_all | solution.py:171
  48.3 8.8 %all-to-all-start.1 = ((f32[16,256,128]{2,0,1:T(8,128)}), f32[16,256,128]{2,0,1:T(8,128)S(1)}, u32[]{:S(2)}, u32[]{:S(2)}) async-start(f32[16,256,128]{2,0,1:T(8,128)} %multiply_bitcast_fusion), calls=%async_computation.1 | async-start | bytes 4194304 | tf_op jit(solution)/shard_map/all_to_all | solution.py:133
  57.9 7.3 %reduce.4 = f32[4,98304]{1,0:T(4,128)} reduce(f32[4,1,98304]{2,1,0:T(1,128)} %all-to-all-done, f32[]{:T(128)} %broadcast.2770), dimensions={1}, to_apply=%all_to_all.14.reduce_sub_computation | reduce | bytes 3145732 | tf_op jit(solution)/shard_map/all_to_all | solution.py:171
  65.2 10.5 %reshape.179 = f32[1024,3,8,16]{3,2,1,0:T(8,128)} reshape(f32[4,98304]{1,0:T(4,128)} %reduce.4) | data formatting | bytes 3145728
  75.7 8.6 %copy.63 = f32[3,8,16,4,256]{4,3,2,1,0:T(4,128)} copy(f32[3,8,16,4,256]{2,1,0,4,3:T(8,128)} %bitcast.238) | data formatting | bytes 3145728 | tf_op jit(solution)/shard_map/all_to_all | solution.py:171
  88.6 3.5 %collective-permute-start.1 = (f32[1,2,8,16,256]{4,3,2,0,1:T(8,128)}, f32[1,2,8,16,256]{4,3,2,0,1:T(8,128)}, u32[]{:S(2)}, u32[]{:S(2)}) collective-permute-start(f32[1,2,8,16,256]{4,3,2,0,1:T(8,128)} %get-tuple-element.98), channel_id=1, source_target_pairs={{0,8},{4,12},{8,0},{12,4},{1,9},{5,13},{9,1},{13,5},{2,10},{6,14},... | collective-permute-start | bytes 786440 | tf_op jit(solution)/shard_map/ppermute | solution.py:30
  94.6 3.4 %collective-permute-done = f32[1,2,8,16,256]{4,3,2,0,1:T(8,128)} collective-permute-done((f32[1,2,8,16,256]{4,3,2,0,1:T(8,128)}, f32[1,2,8,16,256]{4,3,2,0,1:T(8,128)}, u32[]{:S(2)}, u32[]{:S(2)}) %collective-permute-start) | collective-permute-done | bytes 262176 | tf_op jit(solution)/shard_map/ppermute | solution.py:30
  100.8 4.1 %collective-permute-done.2 = f32[1,2,8,16,256]{4,3,2,0,1:T(8,128)} collective-permute-done((f32[1,2,8,16,256]{4,3,2,0,1:T(8,128)}, f32[1,2,8,16,256]{4,3,2,0,1:T(8,128)}, u32[]{:S(2)}, u32[]{:S(2)}) %collective-permute-start.2) | collective-permute-done | bytes 262176 | tf_op jit(solution)/shard_map/ppermute | solution.py:30
  105.9 1.7 copy.55
  107.6 1.8 %reshape_reshape.3 = f32[16,16,1024]{2,1,0:T(8,128)S(1)} reshape(f32[2,8,16,4,256]{4,3,2,1,0:T(4,128)} %copy.55) | data formatting | bytes 2097152 | tf_op jit(solution)/shard_map/reshape;reshape | solution.py:101
  109.4 1.7 fusion.137
  111.1 3.7 %fusion.4 = f32[16,128,128]{2,1,0:T(8,128)} fusion(f32[256,128,1]{0,1,2:T(8,128)} %convolution_bitcast_fusion, f32[16,256,128]{2,0,1:T(8,128)S(1)} %all-to-all-done.1), kind=kOutput, calls=%fused_computation.12 | convolution fusion | flops 805306368 | bytes 3276800 | tf_op jit(solution)/shard_map/lic,ib->lbc/dot_general | solution.py:151
  114.8 1.5 reshape.163
  117.4 1.9 %collective-permute-start.4 = (f32[34,1,1024]{2,1,0:T(1,128)S(1)}, f32[34,1,1024]{2,1,0:T(1,128)S(1)}, u32[]{:S(2)}, u32[]{:S(2)}) collective-permute-start(f32[34,1,1024]{2,1,0:T(1,128)S(1)} %get-tuple-element.84), channel_id=1, source_target_pairs={{0,16},{16,32},{32,48},{48,64},{64,80},{80,96},{96,112},{112,128},... | collective-permute-start | bytes 417800 | tf_op jit(solution)/shard_map/ppermute | solution.py:43
  119.3 1.3 collective-permute-start.3
  121.1 2.8 %collective-permute-done.3 = f32[34,1,1024]{2,1,0:T(1,128)S(1)} collective-permute-done((f32[34,1,1024]{2,1,0:T(1,128)S(1)}, f32[34,1,1024]{2,1,0:T(1,128)S(1)}, u32[]{:S(2)}, u32[]{:S(2)}) %collective-permute-start.3) | collective-permute-done | bytes 139296 | tf_op jit(solution)/shard_map/ppermute | solution.py:45
  124.6 1.3 fusion.135
  126.7 6.1 %collective-permute-start.6 = (f32[17,1,1024]{2,1,0:T(1,128)}, f32[17,1,1024]{2,1,0:T(1,128)}, u32[]{:S(2)}, u32[]{:S(2)}) collective-permute-start(f32[17,1,1024]{2,1,0:T(1,128)} %get-tuple-element.88), channel_id=1, source_target_pairs={{0,16},{16,32},{32,48},{48,64},{64,80},{80,96},{96,112},{112,128},... | collective-permute-start | bytes 208904 | tf_op jit(solution)/shard_map/ppermute | solution.py:43
  132.8 1.3 collective-permute-start.5
  134.1 1.7 fusion.35
  135.8 2.2 %reduce_sum.39 = f32[8,16,1024]{2,1,0:T(8,128)} reduce(f32[2,8,16,1024]{3,2,1,0:T(8,128)} %bitcast.272, f32[]{:T(128)} %constant.95.clone.1), dimensions={0}, to_apply=%region_7.8 | reduce | flops 131072 | bytes 1572868 | tf_op jit(solution)/shard_map/reduce_sum | solution.py:183
  138.0 1.2 fusion.2
  140.0 3.0 %collective-permute-start.8 = (f32[17,1,1024]{2,1,0:T(1,128)S(1)}, f32[17,1,1024]{2,1,0:T(1,128)S(1)}, u32[]{:S(2)}, u32[]{:S(2)}) collective-permute-start(f32[17,1,1024]{2,1,0:T(1,128)S(1)} %get-tuple-element.86), channel_id=1, source_target_pairs={{0,16},{16,32},{32,48},{48,64},{64,80},{80,96},{96,112},{112,128},... | collective-permute-start | bytes 208904 | tf_op jit(solution)/shard_map/ppermute | solution.py:43
  143.5 1.3 collective-permute-start.7
  145.1 1.7 collective-permute-done.7
  146.8 1.6 fusion.27
  148.4 18.1 %reduce-scatter.2.cloned.1.call-done = f32[8,16,256]{2,1,0:T(8,128)} async-done(((f32[8,16,1024]{2,1,0:T(8,128)}), f32[8,16,256]{2,1,0:T(8,128)}) %reduce-scatter.2.cloned.1.call-update) | async-done | bytes 131088 | tf_op jit(solution)/shard_map/reduce_scatter | solution.py:182
  (141 shorter events, 22.7 us)
Async XLA Ops:
  23.9 6.7 %copy-start.10 = (s32[16,256]{1,0:T(8,128)S(1)}, s32[16,256]{1,0:T(8,128)}, u32[]{:S(2)}) copy-start(s32[16,256]{1,0:T(8,128)} %param.18) | copy-start | bytes 49156
  23.9 6.7 %copy-start.12 = (s32[16]{0:T(128)S(1)}, s32[16]{0:T(128)}, u32[]{:S(2)}) copy-start(s32[16]{0:T(128)} %param.21) | copy-start | bytes 196
  23.9 6.9 %copy-start.2 = (f32[2,8,16,1024]{3,2,1,0:T(8,128)S(1)}, f32[2,8,16,1024]{3,2,1,0:T(8,128)}, u32[]{:S(2)}) copy-start(f32[2,8,16,1024]{3,2,1,0:T(8,128)} %param.11) | copy-start | bytes 3145732
  23.9 24.4 %all-to-all-start = ((f32[4,1,98304]{2,1,0:T(1,128)}), f32[4,1,98304]{2,1,0:T(1,128)}, u32[]{:S(2)}, u32[]{:S(2)}) async-start(f32[4,1,98304]{2,1,0:T(1,128)} %reshape.178), calls=%async_computation | async-start | bytes 3145728 | tf_op jit(solution)/shard_map/all_to_all | solution.py:171
  30.6 1.2 copy-start.11
  48.3 62.7 %all-to-all-start.1 = ((f32[16,256,128]{2,0,1:T(8,128)}), f32[16,256,128]{2,0,1:T(8,128)S(1)}, u32[]{:S(2)}, u32[]{:S(2)}) async-start(f32[16,256,128]{2,0,1:T(8,128)} %multiply_bitcast_fusion), calls=%async_computation.1 | async-start | bytes 4194304 | tf_op jit(solution)/shard_map/all_to_all | solution.py:133
  57.1 109.4 %reduce-scatter.2.cloned.1.call-start = ((), (), s32[]{:S(2)}) async-start(), calls=%async_computation.3 | async-start | bytes 655360 | tf_op jit(solution)/shard_map/reduce_scatter | solution.py:182
  84.2 1.6 copy-start.1
  87.5 7.0 %copy-start.7 = (f32[16,1024]{1,0:T(8,128)S(1)}, f32[16,1024]{1,0:T(8,128)}, u32[]{:S(2)}) copy-start(f32[16,1024]{1,0:T(8,128)} %param.16) | copy-start | bytes 196612
  87.5 7.0 %copy-start.9 = (f32[16,1024]{1,0:T(8,128)S(1)}, f32[16,1024]{1,0:T(8,128)}, u32[]{:S(2)}) copy-start(f32[16,1024]{1,0:T(8,128)} %param.14) | copy-start | bytes 196612
  88.6 9.4 %collective-permute-start = (f32[1,2,8,16,256]{4,3,2,0,1:T(8,128)}, f32[1,2,8,16,256]{4,3,2,0,1:T(8,128)}, u32[]{:S(2)}, u32[]{:S(2)}) collective-permute-start(f32[1,2,8,16,256]{4,3,2,0,1:T(8,128)} %get-tuple-element.99), channel_id=1, source_target_pairs={{0,4},{4,8},{8,12},{12,0},{1,5},{5,9},{9,13},{13,1},{2,6},{6,10},{... | collective-permute-start | bytes 786440 | tf_op jit(solution)/shard_map/ppermute | solution.py:30
  88.6 11.2 %collective-permute-start.1 = (f32[1,2,8,16,256]{4,3,2,0,1:T(8,128)}, f32[1,2,8,16,256]{4,3,2,0,1:T(8,128)}, u32[]{:S(2)}, u32[]{:S(2)}) collective-permute-start(f32[1,2,8,16,256]{4,3,2,0,1:T(8,128)} %get-tuple-element.98), channel_id=1, source_target_pairs={{0,8},{4,12},{8,0},{12,4},{1,9},{5,13},{9,1},{13,5},{2,10},{6,14},... | collective-permute-start | bytes 786440 | tf_op jit(solution)/shard_map/ppermute | solution.py:30
  92.8 12.2 %collective-permute-start.2 = (f32[1,2,8,16,256]{4,3,2,0,1:T(8,128)}, f32[1,2,8,16,256]{4,3,2,0,1:T(8,128)}, u32[]{:S(2)}, u32[]{:S(2)}) collective-permute-start(f32[1,2,8,16,256]{4,3,2,0,1:T(8,128)} %get-tuple-element.97), channel_id=1, source_target_pairs={{0,12},{4,0},{8,4},{12,8},{1,13},{5,1},{9,5},{13,9},{2,14},{6,2},{... | collective-permute-start | bytes 786440 | tf_op jit(solution)/shard_map/ppermute | solution.py:30
  114.8 1.5 copy-start.8
  116.3 0.8 copy-start
  116.3 0.9 copy-start.6
  117.4 3.6 %collective-permute-start.4 = (f32[34,1,1024]{2,1,0:T(1,128)S(1)}, f32[34,1,1024]{2,1,0:T(1,128)S(1)}, u32[]{:S(2)}, u32[]{:S(2)}) collective-permute-start(f32[34,1,1024]{2,1,0:T(1,128)S(1)} %get-tuple-element.84), channel_id=1, source_target_pairs={{0,16},{16,32},{32,48},{48,64},{64,80},{80,96},{96,112},{112,128},... | collective-permute-start | bytes 417800 | tf_op jit(solution)/shard_map/ppermute | solution.py:43
  119.3 4.5 %collective-permute-start.3 = (f32[34,1,1024]{2,1,0:T(1,128)S(1)}, f32[34,1,1024]{2,1,0:T(1,128)S(1)}, u32[]{:S(2)}, u32[]{:S(2)}) collective-permute-start(f32[34,1,1024]{2,1,0:T(1,128)S(1)} %get-tuple-element.83), channel_id=1, source_target_pairs={{16,0},{32,16},{48,32},{64,48},{80,64},{96,80},{112,96},{128,112},... | collective-permute-start | bytes 417800 | tf_op jit(solution)/shard_map/ppermute | solution.py:45
  124.6 9.5 %copy-start.5 = (f32[16,16,1023]{2,1,0:T(8,128)S(1)}, f32[16,16,1023]{2,1,0:T(8,128)}, u32[]{:S(2)}) copy-start(f32[16,16,1023]{2,1,0:T(8,128)} %get-tuple-element.96) | copy-start | bytes 3142660
  125.9 8.2 %copy-start.4 = (f32[16,16,1023]{2,1,0:T(8,128)S(1)}, f32[16,16,1023]{2,1,0:T(8,128)}, u32[]{:S(2)}) copy-start(f32[16,16,1023]{2,1,0:T(8,128)} %get-tuple-element.95) | copy-start | bytes 3142660
  126.7 11.4 %collective-permute-start.6 = (f32[17,1,1024]{2,1,0:T(1,128)}, f32[17,1,1024]{2,1,0:T(1,128)}, u32[]{:S(2)}, u32[]{:S(2)}) collective-permute-start(f32[17,1,1024]{2,1,0:T(1,128)} %get-tuple-element.88), channel_id=1, source_target_pairs={{0,16},{16,32},{32,48},{48,64},{64,80},{80,96},{96,112},{112,128},... | collective-permute-start | bytes 208904 | tf_op jit(solution)/shard_map/ppermute | solution.py:43
  132.8 6.5 %collective-permute-start.5 = (f32[17,1,1024]{2,1,0:T(1,128)}, f32[17,1,1024]{2,1,0:T(1,128)S(1)}, u32[]{:S(2)}, u32[]{:S(2)}) collective-permute-start(f32[17,1,1024]{2,1,0:T(1,128)} %get-tuple-element.87), channel_id=1, source_target_pairs={{16,0},{32,16},{48,32},{64,48},{80,64},{96,80},{112,96},{128,112},... | collective-permute-start | bytes 208904 | tf_op jit(solution)/shard_map/ppermute | solution.py:45
  138.0 1.3 copy-start.3
  140.0 4.7 %collective-permute-start.8 = (f32[17,1,1024]{2,1,0:T(1,128)S(1)}, f32[17,1,1024]{2,1,0:T(1,128)S(1)}, u32[]{:S(2)}, u32[]{:S(2)}) collective-permute-start(f32[17,1,1024]{2,1,0:T(1,128)S(1)} %get-tuple-element.86), channel_id=1, source_target_pairs={{0,16},{16,32},{32,48},{48,64},{64,80},{80,96},{96,112},{112,128},... | collective-permute-start | bytes 208904 | tf_op jit(solution)/shard_map/ppermute | solution.py:43
  143.5 3.3 %collective-permute-start.7 = (f32[17,1,1024]{2,1,0:T(1,128)S(1)}, f32[17,1,1024]{2,1,0:T(1,128)S(1)}, u32[]{:S(2)}, u32[]{:S(2)}) collective-permute-start(f32[17,1,1024]{2,1,0:T(1,128)S(1)} %get-tuple-element.85), channel_id=1, source_target_pairs={{16,0},{32,16},{48,32},{64,48},{80,64},{96,80},{112,96},{128,112},... | collective-permute-start | bytes 208904 | tf_op jit(solution)/shard_map/ppermute | solution.py:45
Sparse Core Ops, SparseCore 0:
  138.1 28.3 reduce-scatter.1
